TPU v7x, 32 devices: a whole 2x2x4 slice. The times are simulated.
32 devices in a mesh: group: 2 (over y), blk: 4 (over z), head: 4 (over x, core).
Axes of the slice: x: 2, y: 2, z: 4, core: 2. Of those that a mesh axis runs over, the one named last changes fastest.
Arguments:
- query_a: bfloat16 [768, 5120], P(('group', 'blk', 'head')), parts along dimension 0, may hold values from -600 to 600
- key_a: bfloat16 [768, 5120], P(('group', 'blk', 'head')), parts along dimension 0, may hold values from -600 to 600
- value_a: bfloat16 [768, 5120], P(('group', 'blk', 'head')), parts along dimension 0, may hold values from -6 to 6
- query_b: bfloat16 [768, 5120], P(('group', 'blk', 'head')), parts along dimension 0, may hold values from -600 to 600
- key_b: bfloat16 [768, 5120], P(('group', 'blk', 'head')), parts along dimension 0, may hold values from -600 to 600
- value_b: bfloat16 [768, 5120], P(('group', 'blk', 'head')), parts along dimension 0, may hold values from -6 to 6
- query_gain: float32 [5120], replicated, may hold values from 0.8 to 2.5
- key_gain: float32 [5120], replicated, may hold values from 0.8 to 2.5
Outputs:
- attended_a: bfloat16 [768, 5120], P(('group', 'blk', 'head')), parts along dimension 0
- attended_b: bfloat16 [768, 5120], P(('group', 'blk', 'head')), parts along dimension 0
There are 2 independent parts, one for each index of `group`. A program takes and returns all parts, laid end to end along the dimension named above; an argument that names none is the same for every part. Nothing has to cross between parts.
All inputs are finite; a program needn't handle non-finite values. Where the computation divides by a largest or mean magnitude, that divisor is 1e-20 or more.
Results may differ from a plain program's by a relative error of at most 0.001.
The roundings to bfloat16 on the way count: a program that leaves them out, or rounds other values in their place, can miss the bound.
Values may be sent and summed in bfloat16 or wider, within the bound.
A program may use at most 64 MiB of HBM per device.

v0:
```python
import math

import jax
import jax.numpy as jnp
from jax import lax
from jax.sharding import PartitionSpec as P

HEADS = 40
HEAD_DIM = 128


norm_eps = 1e-06


def normalize(values, gain_vec):
    widened = values.astype(jnp.float32)
    inverse = lax.rsqrt(jnp.mean(widened * widened, axis=-1, keepdims=True) + norm_eps)
    return (widened * inverse * gain_vec).astype(jnp.bfloat16)


def to_heads(matrix):
    return matrix.reshape(matrix.shape[0], HEADS, HEAD_DIM)


def binary_scale(magnitude):
    factor_now = jnp.full(magnitude.shape, 2.0 ** (-20), jnp.float32)
    for exponent in range(-20, 10):
        factor_now = factor_now * jnp.where(magnitude >= 2.0**exponent, 2.0, 1.0)
    return factor_now


def coarse_code(ratio):
    step_size = jnp.full(ratio.shape, 2.0 ** (-17), jnp.float32)
    magnitude = jnp.abs(ratio)
    for exponent in range(1, 15):
        step_size = step_size * jnp.where(magnitude >= 2.0 ** (-exponent), 2.0, 1.0)
    return jnp.floor(ratio / step_size + 0.5) * step_size


def block_length(total_rows):
    return max(
        (step_len for step_len in range(1, min(total_rows, 512) + 1) if total_rows % step_len == 0)
    )


def absorb(status, scores, value_rows, precise):
    run_max, run_sum, run_acc = status
    new_max = jnp.maximum(run_max, jnp.max(scores, axis=-1))
    factor = jnp.exp(run_max - new_max)
    weights = jnp.exp(scores - new_max[..., None])
    run_sum = run_sum * factor + jnp.sum(weights, axis=-1)
    if precise:
        update = jnp.einsum("qhk,khd->qhd", weights, value_rows, precision=lax.Precision.HIGHEST)
    else:
        update = jnp.einsum(
            "qhk,khd->qhd",
            weights.astype(jnp.bfloat16),
            value_rows,
            preferred_element_type=jnp.float32,
        )
    return (new_max, run_sum, run_acc * factor[..., None] + update)


def sweep(status, total_rows, block_fn):
    length = block_length(total_rows)

    def one_block(block_no, current):
        return block_fn(current, block_no * length, length)

    return lax.fori_loop(0, total_rows // length, one_block, status)


def rough_blocks(queries, key_rows, value_rows):
    inv_root = 1.0 / math.sqrt(queries.shape[-1])

    def block_fn(current, offset, length):
        key_blk = lax.dynamic_slice_in_dim(key_rows, offset, length, 0)
        value_blk = lax.dynamic_slice_in_dim(value_rows, offset, length, 0)
        scores = (
            jnp.einsum("qhd,khd->qhk", queries, key_blk, preferred_element_type=jnp.float32)
            * inv_root
        )
        return absorb(current, scores, value_blk, False)

    return block_fn


def exact_blocks(queries, cache_keys, cache_values, coded_rows, row_base):
    code_keys, code_values, scale_keys, scale_values = coded_rows
    inv_root = 1.0 / math.sqrt(queries.shape[-1])

    def block_fn(current, offset, length):
        old_keys = lax.dynamic_slice_in_dim(cache_keys, row_base + offset, length, 0).astype(
            jnp.float32
        )
        old_values = lax.dynamic_slice_in_dim(cache_values, row_base + offset, length, 0).astype(
            jnp.float32
        )
        key_scale = lax.dynamic_slice_in_dim(scale_keys, offset, length, 0).astype(jnp.float32)
        value_scale = lax.dynamic_slice_in_dim(scale_values, offset, length, 0).astype(jnp.float32)
        new_keys = old_keys + key_scale[..., None] * lax.dynamic_slice_in_dim(
            code_keys, offset, length, 0
        ).astype(jnp.float32)
        new_values = old_values + value_scale[..., None] * lax.dynamic_slice_in_dim(
            code_values, offset, length, 0
        ).astype(jnp.float32)
        scores = (
            jnp.einsum("qhd,khd->qhk", queries, new_keys, precision=lax.Precision.HIGHEST)
            * inv_root
        )
        return absorb(current, scores, new_values, True)

    return block_fn


def fresh_status(queries):
    leading = queries.shape[:2]
    return (
        jnp.full(leading, -jnp.inf, jnp.float32),
        jnp.zeros(leading, jnp.float32),
        jnp.zeros(queries.shape, jnp.float32),
    )


def finish(status):
    run_max, run_sum, run_acc = status
    return (run_acc / run_sum[..., None]).astype(jnp.bfloat16)


def send_back(result):
    moved = lax.all_to_all(result, "head", split_axis=0, concat_axis=1, tiled=True)
    return moved.reshape(moved.shape[0], moved.shape[1] * moved.shape[2])


def prepare(query, key_rows, value_rows, query_gain, key_gain):
    moved_query, moved_key, moved_value = (
        lax.all_to_all(
            to_heads(normalize(query, query_gain)), "head", split_axis=1, concat_axis=0, tiled=True
        ),
        lax.all_to_all(
            to_heads(normalize(key_rows, key_gain)), "head", split_axis=1, concat_axis=0, tiled=True
        ),
        lax.all_to_all(to_heads(value_rows), "head", split_axis=1, concat_axis=0, tiled=True),
    )
    return (moved_query, moved_key, moved_value)


def shards(query_a, key_a, value_a, query_b, key_b, value_b, query_gain, key_gain):
    queries_a, keys_a, values_a = prepare(query_a, key_a, value_a, query_gain, key_gain)
    queries_b, keys_b, values_b = prepare(query_b, key_b, value_b, query_gain, key_gain)
    total_rows = keys_a.shape[0] * lax.axis_size("blk")
    start_a = fresh_status(queries_a)
    cache_keys, cache_values = (
        lax.all_gather(keys_a, "blk", axis=0, tiled=True),
        lax.all_gather(values_a, "blk", axis=0, tiled=True),
    )
    status_a = sweep(start_a, total_rows, rough_blocks(queries_a, cache_keys, cache_values))
    attended_a = send_back(finish(status_a))
    residual_key = keys_b.astype(jnp.float32) - keys_a.astype(jnp.float32)
    residual_value = values_b.astype(jnp.float32) - values_a.astype(jnp.float32)
    scale_key = binary_scale(jnp.max(jnp.abs(residual_key), axis=-1)).astype(jnp.bfloat16)
    scale_value = binary_scale(jnp.max(jnp.abs(residual_value), axis=-1)).astype(jnp.bfloat16)
    code_key = coarse_code(residual_key / scale_key.astype(jnp.float32)[..., None]).astype(
        jnp.bfloat16
    )
    code_value = coarse_code(residual_value / scale_value.astype(jnp.float32)[..., None]).astype(
        jnp.bfloat16
    )
    queries_wide = queries_b.astype(jnp.float32)
    start_b = fresh_status(queries_b)
    gathered = (
        lax.all_gather(code_key, "blk", axis=0, tiled=True),
        lax.all_gather(code_value, "blk", axis=0, tiled=True),
        lax.all_gather(scale_key, "blk", axis=0, tiled=True),
        lax.all_gather(scale_value, "blk", axis=0, tiled=True),
    )
    status_b = sweep(
        start_b, total_rows, exact_blocks(queries_wide, cache_keys, cache_values, gathered, 0)
    )
    attended_b = send_back(finish(status_b))
    return (attended_a, attended_b)


def solution(mesh):
    return jax.shard_map(
        shards,
        mesh=mesh,
        in_specs=(
            P(("group", "blk", "head"), None),
            P(("group", "blk", "head"), None),
            P(("group", "blk", "head"), None),
            P(("group", "blk", "head"), None),
            P(("group", "blk", "head"), None),
            P(("group", "blk", "head"), None),
            P(),
            P(),
        ),
        out_specs=(P(("group", "blk", "head"), None), P(("group", "blk", "head"), None)),
        check_vma=False,
    )
```

profile of v0, /device:TPU:1, one launch (start us, length us, event | category | flops | bytes accessed | tf_op | source)
XLA Modules:
  0.0 206.8 jit_solution(14927410978750196656)
XLA Ops:
  0.7 1.2 fusion.47
  1.8 1.1 fusion.53
  3.0 1.3 fusion.60
  4.3 0.7 copy.125
  5.0 4.3 %all-to-all-start = ((bf16[24,40,128]{2,0,1:T(8,128)(2,1)}), bf16[24,40,128]{2,0,1:T(8,128)(2,1)S(1)}, u32[]{:S(2)}, u32[]{:S(2)}) async-start(bf16[24,40,128]{2,0,1:T(8,128)(2,1)} %bitcast.195), calls=%async_computation | async-start | bytes 491520 | tf_op jit(solution)/shard_map/all_to_all | solution.py:140
  9.3 0.7 copy.123
  10.6 0.7 copy.122
  11.3 0.7 copy.124
  12.1 0.8 copy_bitcast_fusion.2
  12.8 1.3 all-to-all-done
  14.2 4.3 %all-to-all-start.4 = ((bf16[24,40,128]{2,0,1:T(8,128)(2,1)}), bf16[24,40,128]{2,0,1:T(8,128)(2,1)S(1)}, u32[]{:S(2)}, u32[]{:S(2)}) async-start(bf16[24,40,128]{2,0,1:T(8,128)(2,1)} %bitcast.193), calls=%async_computation.4 | async-start | bytes 491520 | tf_op jit(solution)/shard_map/all_to_all | solution.py:140
  18.5 0.7 copy_bitcast_fusion.5
  19.3 4.2 %all-to-all-done.4 = bf16[24,40,128]{2,0,1:T(8,128)(2,1)S(1)} async-done(((bf16[24,40,128]{2,0,1:T(8,128)(2,1)}), bf16[24,40,128]{2,0,1:T(8,128)(2,1)S(1)}, u32[]{:S(2)}, u32[]{:S(2)}) %all-to-all-start.4) | async-done | bytes 245792 | tf_op jit(solution)/shard_map/all_to_all | solution.py:140
  23.5 4.2 %all-to-all-start.6 = ((bf16[24,40,128]{2,0,1:T(8,128)(2,1)}), bf16[24,40,128]{2,0,1:T(8,128)(2,1)S(1)}, u32[]{:S(2)}, u32[]{:S(2)}) async-start(bf16[24,40,128]{2,0,1:T(8,128)(2,1)} %copy_bitcast_fusion.2), calls=%async_computation.6 | async-start | bytes 491520 | tf_op jit(solution)/shard_map/all_to_all | solution.py:143
  29.8 0.9 multiply_convert_fusion.1
  30.7 20.6 %all_gather.21 = bf16[384,10,128]{2,0,1:T(8,128)(2,1)} all-gather(bf16[96,10,128]{2,0,1:T(8,128)(2,1)S(1)} %multiply_convert_fusion.1), channel_id=1, replica_groups=mesh['group'=2,'blk'=4,'head'=4] {'blk'}, dimensions={0}, use_global_device_ids=true | all-gather | bytes 1228800 | tf_op jit(solution)/shard_map/all_gather | solution.py:172
  51.3 5.8 %all-to-all-start.2 = ((bf16[24,40,128]{2,0,1:T(8,128)(2,1)}), bf16[24,40,128]{2,0,1:T(8,128)(2,1)S(1)}, u32[]{:S(2)}, u32[]{:S(2)}) async-start(bf16[24,40,128]{2,0,1:T(8,128)(2,1)} %copy_bitcast_fusion.5), calls=%async_computation.2 | async-start | bytes 491520 | tf_op jit(solution)/shard_map/all_to_all | solution.py:143
  57.1 19.5 %all_gather.18 = bf16[384,10,128]{2,0,1:T(8,128)(2,1)S(1)} all-gather(bf16[96,10,128]{2,0,1:T(8,128)(2,1)S(1)} %bitcast.197), channel_id=1, replica_groups=mesh['group'=2,'blk'=4,'head'=4] {'blk'}, dimensions={0}, use_global_device_ids=true | all-gather | bytes 1228800 | tf_op jit(solution)/shard_map/all_gather | solution.py:154
  76.6 4.9 %all-to-all-start.5 = ((bf16[24,40,128]{2,0,1:T(8,128)(2,1)}), bf16[24,40,128]{2,0,1:T(8,128)(2,1)S(1)}, u32[]{:S(2)}, u32[]{:S(2)}) async-start(bf16[24,40,128]{2,0,1:T(8,128)(2,1)} %bitcast.192), calls=%async_computation.5 | async-start | bytes 491520 | tf_op jit(solution)/shard_map/all_to_all | solution.py:137
  81.5 10.2 %all-gather = bf16[4,96,10]{1,2,0:T(8,128)(2,1)S(1)} all-gather(bf16[1,96,10]{1,2,0:T(8,128)(2,1)S(1)} %bitcast.213), channel_id=1, replica_groups=mesh['group'=2,'blk'=4,'head'=4] {'blk'}, dimensions={0}, use_global_device_ids=true | all-gather | bytes 9600 | tf_op jit(solution)/shard_map/all_gather | solution.py:174
  92.1 6.9 %all-to-all-start.1 = ((bf16[24,40,128]{2,0,1:T(8,128)(2,1)}), bf16[24,40,128]{2,0,1:T(8,128)(2,1)}, u32[]{:S(2)}, u32[]{:S(2)}) async-start(bf16[24,40,128]{2,0,1:T(8,128)(2,1)} %bitcast.194), calls=%async_computation.1 | async-start | bytes 491520 | tf_op jit(solution)/shard_map/all_to_all | solution.py:137
  99.1 3.2 %bitcast_reduce_fusion = (f32[96,10]{0,1:T(8,128)S(1)}, f32[10,384,96]{1,2,0:T(8,128)S(1)}) fusion(bf16[96,10,128]{2,0,1:T(8,128)(2,1)S(1)} %bitcast.210, bf16[384,10,128]{2,0,1:T(8,128)(2,1)} %all_gather.21, bf16[384,10,128]{2,0,1:T(8,128)(2,1)S(1)} %all_gather.18, f32[384,10]{0,1:T(8,128)S(1)} %reshape.811), kind=kOutput, calls=%fused_computation.11 | convolution fusion | flops 568933440 | bytes 3705600 | tf_op jit(solution)/shard_map/while/body/eval_jaxpr/qhd,khd->qhk/dot_general | solution.py:108
  103.5 0.7 compare_select_fusion.15
  104.3 0.8 copy.86
  105.2 0.8 copy.87
  106.0 0.7 select_n.789
  106.6 0.8 copy.88
  107.4 0.7 select_n.791
  108.1 0.8 copy.89
  108.9 0.7 select_n.793
  109.5 0.8 copy.90
  110.3 0.7 select_n.795
  111.0 0.8 copy.91
  111.7 0.7 select_n.797
  112.4 0.8 copy.92
  113.2 0.7 select_n.799
  113.9 0.8 copy.93
  114.6 0.7 select_n.801
  115.3 0.8 copy.94
  116.1 0.7 select_n.803
  116.8 0.8 copy.95
  118.2 0.8 copy.96
  119.0 0.7 select_n.807
  119.6 0.8 copy.97
  120.4 0.7 select_n.809
  121.1 0.8 copy.98
  121.9 0.7 select_n.811
  122.5 0.8 copy.99
  123.3 0.7 select_n.813
  124.2 0.9 fusion.65
  125.1 0.9 multiply_convert_fusion
  126.1 19.5 %all_gather.23 = bf16[384,10,128]{2,0,1:T(8,128)(2,1)} all-gather(bf16[96,10,128]{2,0,1:T(8,128)(2,1)S(1)} %multiply_convert_fusion), channel_id=1, replica_groups=mesh['group'=2,'blk'=4,'head'=4] {'blk'}, dimensions={0}, use_global_device_ids=true | all-gather | bytes 1228800 | tf_op jit(solution)/shard_map/all_gather | solution.py:173
  145.5 10.6 %all-gather.1 = bf16[4,96,10]{1,2,0:T(8,128)(2,1)S(1)} all-gather(bf16[1,96,10]{1,2,0:T(8,128)(2,1)S(1)} %bitcast.214), channel_id=1, replica_groups=mesh['group'=2,'blk'=4,'head'=4] {'blk'}, dimensions={0}, use_global_device_ids=true | all-gather | bytes 9600 | tf_op jit(solution)/shard_map/all_gather | solution.py:175
  156.2 18.6 %all_gather.19 = bf16[384,10,128]{2,0,1:T(8,128)(2,1)S(1)} all-gather(bf16[96,10,128]{2,0,1:T(8,128)(2,1)S(1)} %bitcast.196), channel_id=1, replica_groups=mesh['group'=2,'blk'=4,'head'=4] {'blk'}, dimensions={0}, use_global_device_ids=true | all-gather | bytes 1228800 | tf_op jit(solution)/shard_map/all_gather | solution.py:155
  174.8 3.8 %fusion.36 = bf16[96,10,128]{2,0,1:T(8,128)(2,1)S(1)} fusion(f32[10,384,96]{1,2,0:T(8,128)S(1)} %get-tuple-element.111, bf16[384,10,128]{2,0,1:T(8,128)(2,1)} %all_gather.23, bf16[384,10,128]{2,0,1:T(8,128)(2,1)S(1)} %all_gather.19, f32[384,10]{0,1:T(8,128)S(1)} %reshape.813, f32[96,10]{0,1:T(8,128)S(1)} %get-tuple-element.110, f32[96,10]{0,1:T(8,128)S(1)} %copy-done.8, ...), kind=kOutput, calls=%fused_computation.27 | convolution fusion | flops 568934400 | bytes 3713280 | tf_op jit(solution)/shard_map/while/body/eval_jaxpr/qhk,khd->qhd/dot_general | solution.py:53
  178.6 0.9 copy.104
  179.5 9.0 %all-to-all-start.7 = ((bf16[96,10,128]{2,1,0:T(8,128)(2,1)}), bf16[96,10,128]{2,1,0:T(8,128)(2,1)S(1)}, u32[]{:S(2)}, u32[]{:S(2)}) async-start(bf16[96,10,128]{2,1,0:T(8,128)(2,1)} %copy.104), calls=%async_computation.7 | async-start | bytes 786432 | tf_op jit(solution)/shard_map/all_to_all | solution.py:131
  188.5 1.0 copy.57
  191.3 0.9 copy.60
  192.1 2.9 %all-to-all-done.7 = bf16[96,10,128]{2,1,0:T(8,128)(2,1)S(1)} async-done(((bf16[96,10,128]{2,1,0:T(8,128)(2,1)}), bf16[96,10,128]{2,1,0:T(8,128)(2,1)S(1)}, u32[]{:S(2)}, u32[]{:S(2)}) %all-to-all-start.7) | async-done | bytes 245792 | tf_op jit(solution)/shard_map/all_to_all | solution.py:131
  195.1 4.3 %all-to-all-start.3 = ((bf16[96,10,128]{2,1,0:T(8,128)(2,1)}), bf16[96,10,128]{2,1,0:T(8,128)(2,1)S(1)}, u32[]{:S(2)}, u32[]{:S(2)}) async-start(bf16[96,10,128]{2,1,0:T(8,128)(2,1)} %copy.60), calls=%async_computation.3 | async-start | bytes 786432 | tf_op jit(solution)/shard_map/all_to_all | solution.py:131
  199.4 0.9 reshape.783
  200.3 5.7 %all-to-all-done.3 = bf16[96,10,128]{2,1,0:T(8,128)(2,1)S(1)} async-done(((bf16[96,10,128]{2,1,0:T(8,128)(2,1)}), bf16[96,10,128]{2,1,0:T(8,128)(2,1)S(1)}, u32[]{:S(2)}, u32[]{:S(2)}) %all-to-all-start.3) | async-done | bytes 245792 | tf_op jit(solution)/shard_map/all_to_all | solution.py:131
  206.0 0.9 reshape.779
  (92 shorter events, 7.1 us)
Async XLA Ops:
  0.6 11.5 %copy-start = (bf16[24,5120]{1,0:T(8,128)(2,1)S(1)}, bf16[24,5120]{1,0:T(8,128)(2,1)}, u32[]{:S(2)}) copy-start(bf16[24,5120]{1,0:T(8,128)(2,1)} %param.13) | copy-start | bytes 737284
  0.6 9.4 %copy-start.4 = (bf16[24,5120]{1,0:T(8,128)(2,1)S(1)}, bf16[24,5120]{1,0:T(8,128)(2,1)}, u32[]{:S(2)}) copy-start(bf16[24,5120]{1,0:T(8,128)(2,1)} %param.8) | copy-start | bytes 737284
  1.8 8.4 %copy-start.3 = (bf16[24,5120]{1,0:T(8,128)(2,1)S(1)}, bf16[24,5120]{1,0:T(8,128)(2,1)}, u32[]{:S(2)}) copy-start(bf16[24,5120]{1,0:T(8,128)(2,1)} %param.11) | copy-start | bytes 737284
  3.0 7.4 %copy-start.6 = (f32[5120]{0:T(1024)S(1)}, f32[5120]{0:T(1024)}, u32[]{:S(2)}) copy-start(f32[5120]{0:T(1024)} %param.14) | copy-start | bytes 61444
  5.0 9.2 %all-to-all-start = ((bf16[24,40,128]{2,0,1:T(8,128)(2,1)}), bf16[24,40,128]{2,0,1:T(8,128)(2,1)S(1)}, u32[]{:S(2)}, u32[]{:S(2)}) async-start(bf16[24,40,128]{2,0,1:T(8,128)(2,1)} %bitcast.195), calls=%async_computation | async-start | bytes 491520 | tf_op jit(solution)/shard_map/all_to_all | solution.py:140
  10.4 8.1 %copy-start.5 = (bf16[24,5120]{1,0:T(8,128)(2,1)S(1)}, bf16[24,5120]{1,0:T(8,128)(2,1)}, u32[]{:S(2)}) copy-start(bf16[24,5120]{1,0:T(8,128)(2,1)} %param.10) | copy-start | bytes 737284
  14.2 9.3 %all-to-all-start.4 = ((bf16[24,40,128]{2,0,1:T(8,128)(2,1)}), bf16[24,40,128]{2,0,1:T(8,128)(2,1)S(1)}, u32[]{:S(2)}, u32[]{:S(2)}) async-start(bf16[24,40,128]{2,0,1:T(8,128)(2,1)} %bitcast.193), calls=%async_computation.4 | async-start | bytes 491520 | tf_op jit(solution)/shard_map/all_to_all | solution.py:140
  23.5 27.8 %all-to-all-start.6 = ((bf16[24,40,128]{2,0,1:T(8,128)(2,1)}), bf16[24,40,128]{2,0,1:T(8,128)(2,1)S(1)}, u32[]{:S(2)}, u32[]{:S(2)}) async-start(bf16[24,40,128]{2,0,1:T(8,128)(2,1)} %copy_bitcast_fusion.2), calls=%async_computation.6 | async-start | bytes 491520 | tf_op jit(solution)/shard_map/all_to_all | solution.py:143
  51.3 25.3 %all-to-all-start.2 = ((bf16[24,40,128]{2,0,1:T(8,128)(2,1)}), bf16[24,40,128]{2,0,1:T(8,128)(2,1)S(1)}, u32[]{:S(2)}, u32[]{:S(2)}) async-start(bf16[24,40,128]{2,0,1:T(8,128)(2,1)} %copy_bitcast_fusion.5), calls=%async_computation.2 | async-start | bytes 491520 | tf_op jit(solution)/shard_map/all_to_all | solution.py:143
  76.6 15.5 %all-to-all-start.5 = ((bf16[24,40,128]{2,0,1:T(8,128)(2,1)}), bf16[24,40,128]{2,0,1:T(8,128)(2,1)S(1)}, u32[]{:S(2)}, u32[]{:S(2)}) async-start(bf16[24,40,128]{2,0,1:T(8,128)(2,1)} %bitcast.192), calls=%async_computation.5 | async-start | bytes 491520 | tf_op jit(solution)/shard_map/all_to_all | solution.py:137
  92.1 87.4 %all-to-all-start.1 = ((bf16[24,40,128]{2,0,1:T(8,128)(2,1)}), bf16[24,40,128]{2,0,1:T(8,128)(2,1)}, u32[]{:S(2)}, u32[]{:S(2)}) async-start(bf16[24,40,128]{2,0,1:T(8,128)(2,1)} %bitcast.194), calls=%async_computation.1 | async-start | bytes 491520 | tf_op jit(solution)/shard_map/all_to_all | solution.py:137
  126.0 48.7 %copy-start.7 = (f32[96,10]{0,1:T(8,128)S(1)}, f32[96,10]{0,1:T(8,128)}, u32[]{:S(2)}) copy-start(f32[96,10]{0,1:T(8,128)} %get-tuple-element.104) | copy-start | bytes 11524
  126.0 48.7 %copy-start.8 = (f32[96,10]{0,1:T(8,128)S(1)}, f32[96,10]{0,1:T(8,128)}, u32[]{:S(2)}) copy-start(f32[96,10]{0,1:T(8,128)} %get-tuple-element.105) | copy-start | bytes 11524
  174.8 3.8 %copy-start.1 = (bf16[384,10,128]{2,0,1:T(8,128)(2,1)}, bf16[384,10,128]{2,0,1:T(8,128)(2,1)S(1)}, u32[]{:S(2)}) copy-start(bf16[384,10,128]{2,0,1:T(8,128)(2,1)S(1)} %all_gather.19) | copy-start | bytes 2949124
  179.5 15.6 %all-to-all-start.7 = ((bf16[96,10,128]{2,1,0:T(8,128)(2,1)}), bf16[96,10,128]{2,1,0:T(8,128)(2,1)S(1)}, u32[]{:S(2)}, u32[]{:S(2)}) async-start(bf16[96,10,128]{2,1,0:T(8,128)(2,1)} %copy.104), calls=%async_computation.7 | async-start | bytes 786432 | tf_op jit(solution)/shard_map/all_to_all | solution.py:131
  189.5 1.2 copy-start.2
  195.1 10.9 %all-to-all-start.3 = ((bf16[96,10,128]{2,1,0:T(8,128)(2,1)}), bf16[96,10,128]{2,1,0:T(8,128)(2,1)S(1)}, u32[]{:S(2)}, u32[]{:S(2)}) async-start(bf16[96,10,128]{2,1,0:T(8,128)(2,1)} %copy.60), calls=%async_computation.3 | async-start | bytes 786432 | tf_op jit(solution)/shard_map/all_to_all | solution.py:131
where the time goes:
time: 210 us; the launch traced here: 207 us
  blocking collectives  99 us (47%)
  starting transfers between devices  43.7 us (21%)
  local copies, waits for them, and re-layouts  30.7 us (15%)
  waiting for transfers between devices  14.2 us (7%)
  other arithmetic  10 us (5%)
  matrix products  8.25 us (4%)
    select_n x64, local copies, waits for them, and re-layouts, binary_scale(): factor_now = factor_now * jnp.where(magnitude >= 2.0 ** exponent, 2.0, 1.0)  21.2 us
    all_gather x1, blocking collectives, shards(): lax.all_gather(code_key, 'blk', axis=0, tiled=True)  20.6 us
    all_gather x1, blocking collectives, shards(): lax.all_gather(keys_a, 'blk', axis=0, tiled=True)  19.5 us
    all_gather x1, blocking collectives, shards(): lax.all_gather(code_value, 'blk', axis=0, tiled=True)  19.5 us
    all_gather x1, blocking collectives, shards(): lax.all_gather(values_a, 'blk', axis=0, tiled=True)  18.6 us
    all_to_all x2, starting transfers between devices, send_back(): lax.all_to_all(result, 'head', split_axis=0, concat_axis=1, tiled=True)  13.3 us
    all_to_all x2, starting transfers between devices, prepare(): lax.all_to_all(to_heads(normalize(query, query_gain)), 'head', split_axis...  11.8 us
    all_gather x1, blocking collectives, shards(): lax.all_gather(scale_value, 'blk', axis=0, tiled=True)  10.6 us
  transfers between devices with their start and end apart: 8, of which 4 were waited for; matrix products, arithmetic and copies ran while one was open for 21% of the time, Pallas kernels for 0%

commit v1 on v0

--- a/solution.py
+++ b/solution.py
@@ -1,8 +1,11 @@
+import functools
 import math
 
 import jax
 import jax.numpy as jnp
 from jax import lax
+from jax.experimental import pallas as pl
+from jax.experimental.pallas import tpu as pltpu
 from jax.sharding import PartitionSpec as P
 
 HEADS = 40
@@ -181,9 +184,290 @@
     return (attended_a, attended_b)
 
 
+MESH = pl.DeviceIdType.MESH
+
+
+def stepped_code(ratio):
+    magnitude = jnp.abs(ratio)
+    step_size = jnp.full(ratio.shape, 2.0 ** (-17), jnp.float32)
+    inverse = jnp.full(ratio.shape, 2.0**17, jnp.float32)
+    for exponent in range(14, 0, -1):
+        reached = magnitude >= 2.0 ** (-exponent)
+        step_size = jnp.where(reached, 2.0 ** (-2 - exponent), step_size)
+        inverse = jnp.where(reached, 2.0 ** (2 + exponent), inverse)
+    return jnp.floor(ratio * inverse + 0.5) * step_size
+
+
+def coded_residual(fresh, cached):
+    residual = fresh - cached
+    magnitude = jnp.max(jnp.abs(residual), axis=-1, keepdims=True)
+    scale = jnp.full(magnitude.shape, 2.0 ** (-20), jnp.float32)
+    inverse = jnp.full(magnitude.shape, 2.0**20, jnp.float32)
+    for exponent in range(-20, 10):
+        reached = magnitude >= 2.0**exponent
+        scale = jnp.where(reached, 2.0 ** (exponent + 1), scale)
+        inverse = jnp.where(reached, 2.0 ** (-exponent - 1), inverse)
+    return stepped_code(residual * inverse) * scale
+
+
+def fused_kernel(
+    sizes, qa, ka, va, qb, kb, vb, q_gain, k_gain, out_a, out_b,
+    send_a, send_b, got_a, got_b, twin_a, twin_b, back_a, back_b,
+    ssem, rsem, tsem, usem, osem, psem,
+):
+    blks, lanes, own_heads = sizes
+    half_lanes = lanes // 2
+    peers = blks * half_lanes
+    rows, width = qa.shape
+    span = own_heads * HEAD_DIM
+    blk, lane = lax.axis_index("blk"), lax.axis_index("head")
+    side, core = lane // 2, lane % 2
+    me = blk * half_lanes + side
+    here = {"group": lax.axis_index("group")}
+
+    def place(peer):
+        return {**here, "blk": peer // half_lanes, "head": (peer % half_lanes) * 2 + core}
+
+    twin = {**here, "blk": blk, "head": side * 2 + 1 - core}
+
+    def target(i):
+        return (me + i + 1) % peers
+
+    def source(i):
+        return (me + 2 * peers - 1 - i) % peers
+
+    barrier = pltpu.get_barrier_semaphore()
+
+    @pl.loop(0, peers - 1)
+    def _(i):
+        pl.semaphore_signal(barrier, inc=1, device_id=place(target(i)), device_id_type=MESH)
+
+    pl.semaphore_signal(barrier, inc=1, device_id=twin, device_id_type=MESH)
+
+    def columns(start):
+        return pl.ds(pl.multiple_of(start, HEAD_DIM), HEAD_DIM)
+
+    def inverse_norm(ref):
+        def add(h, total):
+            piece = ref[:, columns(h * HEAD_DIM)].astype(jnp.float32)
+            return total + piece * piece
+
+        total = lax.fori_loop(
+            0, width // HEAD_DIM, add, jnp.zeros((rows, HEAD_DIM), jnp.float32), unroll=8
+        )
+        mean = jnp.sum(total, axis=-1, keepdims=True) * (1.0 / width)
+        return lax.rsqrt(mean + norm_eps)
+
+    inv_qa, inv_ka = inverse_norm(qa), inverse_norm(ka)
+    inv_qb, inv_kb = inverse_norm(qb), inverse_norm(kb)
+    pl.semaphore_wait(barrier, peers)
+
+    def normed(ref, inverse, gain, cols):
+        piece = ref[:, cols].astype(jnp.float32)
+        return (piece * inverse * gain[:, cols]).astype(jnp.bfloat16)
+
+    def fill_a(dest, slot, peer):
+        for h in range(own_heads):
+            cols, local = columns(peer * span + h * HEAD_DIM), pl.ds(h * HEAD_DIM, HEAD_DIM)
+            dest[slot, 0, :, local] = normed(qa, inv_qa, q_gain, cols)
+            dest[slot, 1, :, local] = normed(ka, inv_ka, k_gain, cols)
+            dest[slot, 2, :, local] = va[:, cols]
+
+    def fill_b(dest, slot, peer):
+        for h in range(own_heads):
+            cols, local = columns(peer * span + h * HEAD_DIM), pl.ds(h * HEAD_DIM, HEAD_DIM)
+            dest[slot, 0, :, local] = normed(qb, inv_qb, q_gain, cols)
+            fresh = normed(kb, inv_kb, k_gain, cols).astype(jnp.float32)
+            cached = normed(ka, inv_ka, k_gain, cols).astype(jnp.float32)
+            dest[slot, 1, :, local] = coded_residual(fresh, cached).astype(jnp.bfloat16)
+            dest[slot, 2, :, local] = coded_residual(
+                vb[:, cols].astype(jnp.float32), va[:, cols].astype(jnp.float32)
+            ).astype(jnp.bfloat16)
+
+    def forth(step, send, got, peer, slot):
+        return pltpu.make_async_remote_copy(
+            src_ref=send.at[peer],
+            dst_ref=got.at[slot],
+            send_sem=ssem.at[step, peer],
+            recv_sem=rsem.at[step, slot],
+            device_id=place(peer),
+            device_id_type=MESH,
+        )
+
+    def across(step, got, other, slot):
+        return pltpu.make_async_remote_copy(
+            src_ref=got.at[slot, pl.ds(1, 2)],
+            dst_ref=other.at[slot],
+            send_sem=tsem.at[step, slot],
+            recv_sem=usem.at[step, slot],
+            device_id=twin,
+            device_id_type=MESH,
+        )
+
+    def home(step, back, out, peer, slot):
+        return pltpu.make_async_remote_copy(
+            src_ref=back.at[peer],
+            dst_ref=out.at[slot],
+            send_sem=osem.at[step, peer],
+            recv_sem=psem.at[step, slot],
+            device_id=place(peer),
+            device_id_type=MESH,
+        )
+
+    @pl.loop(0, peers - 1)
+    def _(i):
+        peer = target(i)
+        fill_a(send_a, peer, peer)
+        forth(0, send_a, got_a, peer, me).start()
+
+    fill_a(got_a, me, me)
+    across(0, got_a, twin_a, me).start()
+
+    @pl.loop(0, peers - 1)
+    def _(i):
+        peer = target(i)
+        fill_b(send_b, peer, peer)
+        forth(1, send_b, got_b, peer, me).start()
+
+    fill_b(got_b, me, me)
+    across(1, got_b, twin_b, me).start()
+
+    inv_root = 1.0 / math.sqrt(HEAD_DIM)
+
+    def collect(step, send, got, other):
+        @pl.loop(0, peers - 1)
+        def _(i):
+            slot = source(i)
+            forth(step, send, got, slot, slot).wait_recv()
+            across(step, got, other, slot).start()
+
+        @pl.loop(0, peers)
+        def _(slot):
+            across(step, got, other, slot).wait_recv()
+
+    def gather_rows(got, other, part, cols):
+        own = got[:, part, :, cols].astype(jnp.float32).reshape(peers * rows, HEAD_DIM)
+        far = other[:, part - 1, :, cols].astype(jnp.float32).reshape(peers * rows, HEAD_DIM)
+        return jnp.concatenate([own, far], axis=0).astype(jnp.bfloat16)
+
+    def query_rows(got, cols):
+        own = got[:, 0, :, cols].astype(jnp.float32).reshape(peers * rows, HEAD_DIM)
+        return own.astype(jnp.bfloat16)
+
+    def scores_of(queries, keys):
+        return (
+            lax.dot_general(
+                queries, keys, (((1,), (1,)), ((), ())), preferred_element_type=jnp.float32
+            )
+            * inv_root
+        )
+
+    def store_head(back, cols, result):
+        back[:, :, cols] = result.reshape(peers, rows, HEAD_DIM).astype(jnp.bfloat16)
+
+    def send_home(step, back, out):
+        @pl.loop(0, peers - 1)
+        def _(i):
+            home(step, back, out, target(i), me).start()
+
+        out[me] = back[me]
+
+    collect(0, send_a, got_a, twin_a)
+
+    @pl.loop(0, own_heads)
+    def _(h):
+        cols = columns(h * HEAD_DIM)
+        scores = scores_of(query_rows(got_a, cols), gather_rows(got_a, twin_a, 1, cols))
+        weights = jnp.exp(scores - jnp.max(scores, axis=1, keepdims=True))
+        total = jnp.sum(weights, axis=1, keepdims=True)
+        values = gather_rows(got_a, twin_a, 2, cols)
+        mixed = jnp.dot(weights.astype(jnp.bfloat16), values, preferred_element_type=jnp.float32)
+        store_head(back_a, cols, mixed / total)
+
+    send_home(0, back_a, out_a)
+    collect(1, send_b, got_b, twin_b)
+
+    @pl.loop(0, own_heads)
+    def _(h):
+        cols = columns(h * HEAD_DIM)
+        queries = query_rows(got_b, cols)
+        keys = jnp.concatenate(
+            [gather_rows(got_a, twin_a, 1, cols), gather_rows(got_b, twin_b, 1, cols)], axis=1
+        )
+        scores = scores_of(jnp.concatenate([queries, queries], axis=1), keys)
+        weights = jnp.exp(scores - jnp.max(scores, axis=1, keepdims=True))
+        total = jnp.sum(weights, axis=1, keepdims=True)
+        values = jnp.concatenate(
+            [gather_rows(got_a, twin_a, 2, cols), gather_rows(got_b, twin_b, 2, cols)], axis=1
+        )
+        coarse = weights.astype(jnp.bfloat16)
+        fine = (weights - coarse.astype(jnp.float32)).astype(jnp.bfloat16)
+        mixed = jnp.dot(coarse, values, preferred_element_type=jnp.float32) + jnp.dot(
+            fine, values, preferred_element_type=jnp.float32
+        )
+        store_head(back_b, cols, (mixed[:, :HEAD_DIM] + mixed[:, HEAD_DIM:]) / total)
+
+    send_home(1, back_b, out_b)
+
+    for step, send, got, other, back, out in (
+        (0, send_a, got_a, twin_a, back_a, out_a),
+        (1, send_b, got_b, twin_b, back_b, out_b),
+    ):
+
+        @pl.loop(0, peers - 1)
+        def _(i):
+            peer = target(i)
+            forth(step, send, got, peer, me).wait_send()
+            home(step, back, out, peer, me).wait_send()
+
+        @pl.loop(0, peers)
+        def _(slot):
+            across(step, got, other, slot).wait_send()
+
+    for step, back, out in ((0, back_a, out_a), (1, back_b, out_b)):
+
+        @pl.loop(0, peers - 1)
+        def _(i):
+            slot = source(i)
+            home(step, back, out, slot, slot).wait_recv()
+
+
+def fused(sizes):
+    blks, lanes, own_heads = sizes
+    peers = blks * lanes // 2
+    span = own_heads * HEAD_DIM
+
+    def run(qa, ka, va, qb, kb, vb, q_gain, k_gain):
+        rows, width = qa.shape
+        vmem = pl.BlockSpec(memory_space=pltpu.VMEM)
+        block = jax.ShapeDtypeStruct((peers, rows, span), jnp.bfloat16)
+        parts = pltpu.VMEM((peers, 3, rows, span), jnp.bfloat16)
+        pairs = pltpu.VMEM((peers, 2, rows, span), jnp.bfloat16)
+        whole = pltpu.VMEM((peers, rows, span), jnp.bfloat16)
+        sem = pltpu.SemaphoreType.DMA((2, peers))
+        outs = pl.pallas_call(
+            functools.partial(fused_kernel, sizes),
+            out_shape=(block, block),
+            in_specs=[vmem] * 8,
+            out_specs=(vmem, vmem),
+            scratch_shapes=[parts] * 4 + [pairs] * 2 + [whole] * 2 + [sem] * 6,
+            compiler_params=pltpu.CompilerParams(
+                collective_id=0, has_side_effects=True, vmem_limit_bytes=40 * 1024 * 1024
+            ),
+        )(qa, ka, va, qb, kb, vb, q_gain.reshape(1, width), k_gain.reshape(1, width))
+        return tuple(jnp.transpose(o, (1, 0, 2)).reshape(rows, width) for o in outs)
+
+    return run
+
+
 def solution(mesh):
+    blks, lanes = mesh.shape["blk"], mesh.shape["head"]
+    if lanes % 2 == 0 and HEADS % (blks * lanes // 2) == 0:
+        body = fused((blks, lanes, HEADS // (blks * lanes // 2)))
+    else:
+        body = shards
     return jax.shard_map(
-        shards,
+        body,
         mesh=mesh,
         in_specs=(
             P(("group", "blk", "head"), None),

time: 210 us -> 61.8 us (0.29); the launches traced: 207 us -> 61.4 us
  blocking collectives: 99 us -> 0 us
  Pallas kernels: 0 us -> 52.2 us
  starting transfers between devices: 43.7 us -> 0 us
  local copies, waits for them, and re-layouts: 30.7 us -> 8.54 us
  waiting for transfers between devices: 14.2 us -> 0 us
  other arithmetic: 10 us -> 0 us
  matrix products: 8.25 us -> 0 us
    all_gather x6 -> x0, blocking collectives: 99 us -> none  [the longest x1 20.6 us: shards(): lax.all_gather(code_key, 'blk', axis=0, tiled=True)]
    pallas_call x0 -> x1, Pallas kernels: none -> 52.2 us  [run(): pl.pallas_call(functools.partial(fused_kernel, sizes), out_shape=(block,...]
    all_to_all x8 -> x0, starting transfers between devices: 43.7 us -> none  [the longest x2 13.3 us: send_back(): lax.all_to_all(result, 'head', split_axis=0, concat_axis=1, tiled=True)]
    select_n x64 -> x0, local copies, waits for them, and re-layouts: 21.2 us -> none  [binary_scale(): factor_now = factor_now * jnp.where(magnitude >= 2.0 ** exponent, 2.0, 1.0)]
    all_to_all x8 -> x0, waiting for transfers between devices: 14.2 us -> none  [the longest x2 8.6 us: send_back(): lax.all_to_all(result, 'head', split_axis=0, concat_axis=1, tiled=True)]
    dot_general x4 -> x0, matrix products: 8.25 us -> none  [the longest x1 3.8 us: absorb(): jnp.einsum('qhk,khd->qhd', weights, value_rows, precision=lax.Precision.H...]
    unnamed x18 -> x16, local copies, waits for them, and re-layouts: 0.05 us -> 7.11 us
    reshape x8 -> x2, local copies, waits for them, and re-layouts: 6.13 us -> 1.43 us  [run(): jnp.transpose(o, (1, 0, 2)).reshape(rows, width)]
  transfers between devices with their start and end apart: 8 -> 0, of which waited for: 4 -> 0; matrix products, arithmetic and copies ran while one was open for 21% -> 0% of each run, Pallas kernels for 0% -> 0%
where the time goes in v1:
time: 61.8 us; the launch traced here: 61.4 us
  Pallas kernels  52.2 us (84%)
  local copies, waits for them, and re-layouts  8.54 us (14%)
  between operations  0.66 us (1%)
    pallas_call x1, Pallas kernels, run(): pl.pallas_call(functools.partial(fused_kernel, sizes), out_shape=(block,...  52.2 us
    unnamed x16, local copies, waits for them, and re-layouts  7.11 us
    reshape x2, local copies, waits for them, and re-layouts, run(): jnp.transpose(o, (1, 0, 2)).reshape(rows, width)  1.43 us

profile of v1, /device:TPU:1, one launch (start us, length us, event | category | flops | bytes accessed | tf_op | source)
XLA Modules:
  0.0 61.4 jit_solution(16599446679137892471)
XLA Ops:
  0.6 0.0 copy-start
  0.6 0.9 %copy-done = bf16[24,5120]{1,0:T(8,128)(2,1)S(1)} copy-done((bf16[24,5120]{1,0:T(8,128)(2,1)S(1)}, bf16[24,5120]{1,0:T(8,128)(2,1)}, u32[]{:S(2)}) %copy-start) | copy-done | bytes 245784
  1.6 0.0 copy-start.1
  1.6 0.9 %copy-done.1 = bf16[24,5120]{1,0:T(8,128)(2,1)S(1)} copy-done((bf16[24,5120]{1,0:T(8,128)(2,1)S(1)}, bf16[24,5120]{1,0:T(8,128)(2,1)}, u32[]{:S(2)}) %copy-start.1) | copy-done | bytes 245784
  2.5 0.0 copy-start.2
  2.5 0.9 %copy-done.2 = bf16[24,5120]{1,0:T(8,128)(2,1)S(1)} copy-done((bf16[24,5120]{1,0:T(8,128)(2,1)S(1)}, bf16[24,5120]{1,0:T(8,128)(2,1)}, u32[]{:S(2)}) %copy-start.2) | copy-done | bytes 245784
  3.5 0.0 copy-start.3
  3.5 0.9 %copy-done.3 = bf16[24,5120]{1,0:T(8,128)(2,1)S(1)} copy-done((bf16[24,5120]{1,0:T(8,128)(2,1)S(1)}, bf16[24,5120]{1,0:T(8,128)(2,1)}, u32[]{:S(2)}) %copy-start.3) | copy-done | bytes 245784
  4.4 0.0 copy-start.4
  4.4 0.9 %copy-done.4 = bf16[24,5120]{1,0:T(8,128)(2,1)S(1)} copy-done((bf16[24,5120]{1,0:T(8,128)(2,1)S(1)}, bf16[24,5120]{1,0:T(8,128)(2,1)}, u32[]{:S(2)}) %copy-start.4) | copy-done | bytes 245784
  5.4 0.0 copy-start.5
  5.4 0.9 %copy-done.5 = bf16[24,5120]{1,0:T(8,128)(2,1)S(1)} copy-done((bf16[24,5120]{1,0:T(8,128)(2,1)S(1)}, bf16[24,5120]{1,0:T(8,128)(2,1)}, u32[]{:S(2)}) %copy-start.5) | copy-done | bytes 245784
  6.3 0.0 copy-start.6
  6.3 0.7 %copy-done.6 = f32[5120]{0:T(1024)S(1)} copy-done((f32[5120]{0:T(1024)S(1)}, f32[5120]{0:T(1024)}, u32[]{:S(2)}) %copy-start.6) | copy-done | bytes 20504
  7.0 0.0 copy-start.7
  7.0 0.7 %copy-done.7 = f32[5120]{0:T(1024)S(1)} copy-done((f32[5120]{0:T(1024)S(1)}, f32[5120]{0:T(1024)}, u32[]{:S(2)}) %copy-start.7) | copy-done | bytes 20504
  7.8 52.2 %shard_map.95 = (bf16[8,24,640]{2,1,0:T(8,128)(2,1)S(1)}, bf16[8,24,640]{2,1,0:T(8,128)(2,1)S(1)}) custom-call(bf16[24,5120]{1,0:T(8,128)(2,1)S(1)} %copy-done, bf16[24,5120]{1,0:T(8,128)(2,1)S(1)} %copy-done.1, bf16[24,5120]{1,0:T(8,128)(2,1)S(1)} %copy-done.2, bf16[24,5120]{1,0:T(8,128)(2,1)S(1)} %copy-done.3, bf16[24,5120]{1,0:T(8,128)(2,1)S(1)} %copy-done.4, ...), custom_call_target="tpu_custom_call" | custom-call | tf_op jit(solution)/shard_map/pallas_call | solution.py:448
  60.0 0.7 %copy.12 = bf16[8,3,8,640]{3,2,0,1:T(8,128)(2,1)} copy(bf16[8,3,8,640]{3,2,1,0:T(8,128)(2,1)S(1)} %bitcast.9) | data formatting | bytes 491520 | tf_op jit(solution)/shard_map/reshape | solution.py:458
  60.7 0.7 %copy.13 = bf16[8,3,8,640]{3,2,0,1:T(8,128)(2,1)} copy(bf16[8,3,8,640]{3,2,1,0:T(8,128)(2,1)S(1)} %bitcast.8) | data formatting | bytes 491520 | tf_op jit(solution)/shard_map/reshape | solution.py:458
Async XLA Ops:
  0.6 0.9 %copy-start = (bf16[24,5120]{1,0:T(8,128)(2,1)S(1)}, bf16[24,5120]{1,0:T(8,128)(2,1)}, u32[]{:S(2)}) copy-start(bf16[24,5120]{1,0:T(8,128)(2,1)} %qa.1) | copy-start | bytes 737284
  1.6 0.9 %copy-start.1 = (bf16[24,5120]{1,0:T(8,128)(2,1)S(1)}, bf16[24,5120]{1,0:T(8,128)(2,1)}, u32[]{:S(2)}) copy-start(bf16[24,5120]{1,0:T(8,128)(2,1)} %ka.1) | copy-start | bytes 737284
  2.5 0.9 %copy-start.2 = (bf16[24,5120]{1,0:T(8,128)(2,1)S(1)}, bf16[24,5120]{1,0:T(8,128)(2,1)}, u32[]{:S(2)}) copy-start(bf16[24,5120]{1,0:T(8,128)(2,1)} %va.1) | copy-start | bytes 737284
  3.5 0.9 %copy-start.3 = (bf16[24,5120]{1,0:T(8,128)(2,1)S(1)}, bf16[24,5120]{1,0:T(8,128)(2,1)}, u32[]{:S(2)}) copy-start(bf16[24,5120]{1,0:T(8,128)(2,1)} %qb.1) | copy-start | bytes 737284
  4.4 0.9 %copy-start.4 = (bf16[24,5120]{1,0:T(8,128)(2,1)S(1)}, bf16[24,5120]{1,0:T(8,128)(2,1)}, u32[]{:S(2)}) copy-start(bf16[24,5120]{1,0:T(8,128)(2,1)} %kb.1) | copy-start | bytes 737284
  5.4 0.9 %copy-start.5 = (bf16[24,5120]{1,0:T(8,128)(2,1)S(1)}, bf16[24,5120]{1,0:T(8,128)(2,1)}, u32[]{:S(2)}) copy-start(bf16[24,5120]{1,0:T(8,128)(2,1)} %vb.1) | copy-start | bytes 737284
  6.3 0.7 %copy-start.6 = (f32[5120]{0:T(1024)S(1)}, f32[5120]{0:T(1024)}, u32[]{:S(2)}) copy-start(f32[5120]{0:T(1024)} %param.14) | copy-start | bytes 61444
  7.0 0.7 %copy-start.7 = (f32[5120]{0:T(1024)S(1)}, f32[5120]{0:T(1024)}, u32[]{:S(2)}) copy-start(f32[5120]{0:T(1024)} %param.15) | copy-start | bytes 61444

commit v2 on v1

--- a/solution.py
+++ b/solution.py
@@ -211,9 +211,9 @@
 
 
 def fused_kernel(
-    sizes, qa, ka, va, qb, kb, vb, q_gain, k_gain, out_a, out_b,
-    send_a, send_b, got_a, got_b, twin_a, twin_b, back_a, back_b,
-    ssem, rsem, tsem, usem, osem, psem,
+    sizes, qa_far, ka_far, va_far, qb_far, kb_far, vb_far, q_gain_far, k_gain_far, out_a, out_b,
+    qa, ka, va, qb, kb, vb, q_gain, k_gain, send_a, send_b, got_a, got_b, twin_a, twin_b, back_a, back_b,
+    ssem, rsem, tsem, usem, osem, psem, isem, ksem,
 ):
     blks, lanes, own_heads = sizes
     half_lanes = lanes // 2
@@ -236,6 +236,18 @@
     def source(i):
         return (me + 2 * peers - 1 - i) % peers
 
+    loads = [
+        pltpu.make_async_copy(far, near, isem.at[n])
+        for n, (far, near) in enumerate(
+            (
+                (qa_far, qa), (ka_far, ka), (q_gain_far, q_gain), (k_gain_far, k_gain),
+                (va_far, va), (qb_far, qb), (kb_far, kb), (vb_far, vb),
+            )
+        )
+    ]
+    for load in loads:
+        load.start()
+
     barrier = pltpu.get_barrier_semaphore()
 
     @pl.loop(0, peers - 1)
@@ -258,8 +270,11 @@
         mean = jnp.sum(total, axis=-1, keepdims=True) * (1.0 / width)
         return lax.rsqrt(mean + norm_eps)
 
+    for load in loads[:2]:
+        load.wait()
     inv_qa, inv_ka = inverse_norm(qa), inverse_norm(ka)
-    inv_qb, inv_kb = inverse_norm(qb), inverse_norm(kb)
+    for load in loads[2:5]:
+        load.wait()
     pl.semaphore_wait(barrier, peers)
 
     def normed(ref, inverse, gain, cols):
@@ -307,11 +322,18 @@
     def home(step, back, out, peer, slot):
         return pltpu.make_async_remote_copy(
             src_ref=back.at[peer],
-            dst_ref=out.at[slot],
+            dst_ref=out.at[:, pl.ds(pl.multiple_of(slot * span, HEAD_DIM), span)],
             send_sem=osem.at[step, peer],
             recv_sem=psem.at[step, slot],
             device_id=place(peer),
             device_id_type=MESH,
+        )
+
+    def keep(step, back, out):
+        return pltpu.make_async_copy(
+            back.at[me],
+            out.at[:, pl.ds(pl.multiple_of(me * span, HEAD_DIM), span)],
+            ksem.at[step],
         )
 
     @pl.loop(0, peers - 1)
@@ -322,6 +344,10 @@
 
     fill_a(got_a, me, me)
     across(0, got_a, twin_a, me).start()
+
+    for load in loads[5:]:
+        load.wait()
+    inv_qb, inv_kb = inverse_norm(qb), inverse_norm(kb)
 
     @pl.loop(0, peers - 1)
     def _(i):
@@ -364,13 +390,6 @@
 
     def store_head(back, cols, result):
         back[:, :, cols] = result.reshape(peers, rows, HEAD_DIM).astype(jnp.bfloat16)
-
-    def send_home(step, back, out):
-        @pl.loop(0, peers - 1)
-        def _(i):
-            home(step, back, out, target(i), me).start()
-
-        out[me] = back[me]
 
     collect(0, send_a, got_a, twin_a)
 
@@ -384,7 +403,11 @@
         mixed = jnp.dot(weights.astype(jnp.bfloat16), values, preferred_element_type=jnp.float32)
         store_head(back_a, cols, mixed / total)
 
-    send_home(0, back_a, out_a)
+    keep(0, back_a, out_a).start()
+    @pl.loop(0, peers - 1)
+    def _(i):
+        home(0, back_a, out_a, target(i), me).start()
+
     collect(1, send_b, got_b, twin_b)
 
     @pl.loop(0, own_heads)
@@ -407,7 +430,11 @@
         )
         store_head(back_b, cols, (mixed[:, :HEAD_DIM] + mixed[:, HEAD_DIM:]) / total)
 
-    send_home(1, back_b, out_b)
+    @pl.loop(0, peers - 1)
+    def _(i):
+        home(1, back_b, out_b, target(i), me).start()
+
+    keep(1, back_b, out_b).start()
 
     for step, send, got, other, back, out in (
         (0, send_a, got_a, twin_a, back_a, out_a),
@@ -431,6 +458,8 @@
             slot = source(i)
             home(step, back, out, slot, slot).wait_recv()
 
+        keep(step, back, out).wait()
+
 
 def fused(sizes):
     blks, lanes, own_heads = sizes
@@ -439,8 +468,8 @@
 
     def run(qa, ka, va, qb, kb, vb, q_gain, k_gain):
         rows, width = qa.shape
-        vmem = pl.BlockSpec(memory_space=pltpu.VMEM)
-        block = jax.ShapeDtypeStruct((peers, rows, span), jnp.bfloat16)
+        far = pl.BlockSpec(memory_space=pl.ANY)
+        block = jax.ShapeDtypeStruct((rows, width), jnp.bfloat16)
         parts = pltpu.VMEM((peers, 3, rows, span), jnp.bfloat16)
         pairs = pltpu.VMEM((peers, 2, rows, span), jnp.bfloat16)
         whole = pltpu.VMEM((peers, rows, span), jnp.bfloat16)
@@ -448,14 +477,17 @@
         outs = pl.pallas_call(
             functools.partial(fused_kernel, sizes),
             out_shape=(block, block),
-            in_specs=[vmem] * 8,
-            out_specs=(vmem, vmem),
-            scratch_shapes=[parts] * 4 + [pairs] * 2 + [whole] * 2 + [sem] * 6,
+            in_specs=[far] * 8,
+            out_specs=(far, far),
+            scratch_shapes=[pltpu.VMEM((rows, width), jnp.bfloat16)] * 6
+            + [pltpu.VMEM((1, width), jnp.float32)] * 2
+            + [parts] * 4 + [pairs] * 2 + [whole] * 2 + [sem] * 6
+            + [pltpu.SemaphoreType.DMA((8,)), pltpu.SemaphoreType.DMA((2,))],
             compiler_params=pltpu.CompilerParams(
-                collective_id=0, has_side_effects=True, vmem_limit_bytes=40 * 1024 * 1024
+                collective_id=0, has_side_effects=True, vmem_limit_bytes=56 * 1024 * 1024
             ),
         )(qa, ka, va, qb, kb, vb, q_gain.reshape(1, width), k_gain.reshape(1, width))
-        return tuple(jnp.transpose(o, (1, 0, 2)).reshape(rows, width) for o in outs)
+        return tuple(outs)
 
     return run
 

time: 61.8 us -> 55.7 us (0.901)
  local copies, waits for them, and re-layouts: 8.54 us -> 2.39 us
    unnamed x16 -> x4, local copies, waits for them, and re-layouts: 7.11 us -> 2.39 us
    reshape x2 -> x0, local copies, waits for them, and re-layouts: 1.43 us -> none  [run(): jnp.transpose(o, (1, 0, 2)).reshape(rows, width)]
where the time goes in v2:
time: 55.7 us; the launch traced here: 55.5 us
  Pallas kernels  52.5 us (94%)
  local copies, waits for them, and re-layouts  2.39 us (4%)
  between operations  0.65 us (1%)
    pallas_call x1, Pallas kernels, run(): pl.pallas_call(functools.partial(fused_kernel, sizes), out_shape=(block,...  52.5 us
    unnamed x4, local copies, waits for them, and re-layouts  2.39 us

profile of v2, /device:TPU:1, one launch (start us, length us, event | category | flops | bytes accessed | tf_op | source)
XLA Modules:
  0.0 55.5 jit_solution(15020452150911031915)
XLA Ops:
  0.6 52.5 %shard_map.95 = (bf16[24,5120]{1,0:T(8,128)(2,1)}, bf16[24,5120]{1,0:T(8,128)(2,1)}) custom-call(bf16[24,5120]{1,0:T(8,128)(2,1)} %qa_far.1, bf16[24,5120]{1,0:T(8,128)(2,1)} %ka_far.1, bf16[24,5120]{1,0:T(8,128)(2,1)} %va_far.1, bf16[24,5120]{1,0:T(8,128)(2,1)} %qb_far.1, bf16[24,5120]{1,0:T(8,128)(2,1)} %kb_far.1, bf16[24,5120]{1,0:T(8,128)(2,1)} %vb_far.1, ...), custom_call_target="tpu_custom_call" | custom-call | tf_op jit(solution)/shard_map/pallas_call | solution.py:477
  53.1 0.0 copy-start
  53.2 1.7 %copy.12 = bf16[24,5120]{1,0:T(8,128)(2,1)} copy(bf16[24,5120]{1,0:T(8,128)(2,1)} %get-tuple-element.4) | data formatting | bytes 491520
  54.9 0.0 copy-done
  54.9 0.7 %copy.13 = bf16[24,5120]{1,0:T(8,128)(2,1)} copy(bf16[24,5120]{1,0:T(8,128)(2,1)S(1)} %copy-done) | data formatting | bytes 491520
Async XLA Ops:
  53.1 1.7 %copy-start = (bf16[24,5120]{1,0:T(8,128)(2,1)S(1)}, bf16[24,5120]{1,0:T(8,128)(2,1)}, u32[]{:S(2)}) copy-start(bf16[24,5120]{1,0:T(8,128)(2,1)} %get-tuple-element.5) | copy-start | bytes 737284
